TPU v7x, 256 devices: a whole 4x4x8 slice. The times are simulated.
256 devices in a mesh: rows: 64 (over x, z, y_lo), strips: 4 (over y_hi, core).
Axes of the slice: x: 4, y: 4 (y_hi: 2, y_lo: 2; y = y_hi * 2 + y_lo), z: 8, core: 2. Of those that a mesh axis runs over, the one named last changes fastest.
Arguments:
- tokens: bfloat16 [64, 24, 64, 1280], P('rows', None, 'strips'), may hold values from -8 to 8
- stale_kv: bfloat16 [64, 2, 1536, 1280], P('rows', None, 'strips'), may hold values from -180 to 180
- stale_moments: float32 [64, 4, 2, 32], P('rows', 'strips'), as said below
- norm_gain: float32 [1280], replicated, may hold values from 0.1 to 1.9
- norm_bias: float32 [1280], replicated, may hold values from -3 to 3
- w_query: bfloat16 [1280, 1280], P('rows'), may hold values from -0.33398438 to 0.33398438
- w_key: bfloat16 [1280, 1280], P('rows'), may hold values from -0.1953125 to 0.1953125
- w_value: bfloat16 [1280, 1280], P('rows'), may hold values from -0.15625 to 0.15625
- w_out: bfloat16 [1280, 1280], P('rows'), may hold values from -0.33398438 to 0.33398438
Outputs:
- attended: bfloat16 [64, 24, 64, 1280], P('rows', None, 'strips')
- fresh_kv: bfloat16 [64, 2, 1536, 1280], P('rows', None, 'strips')
- fresh_sums: float32 [64, 4, 32], P('rows', 'strips')
- fresh_squares: float32 [64, 4, 32], P('rows', 'strips')
Inputs may be any that keep to these rules, and one draw needn't show every extreme that they name: `stale_moments`: each strip's entries are a sum of 15360 values and the sum of their squares.
All inputs are finite; a program needn't handle non-finite values.
Results may differ from a plain program's by a relative error of at most 0.0075.
The roundings to bfloat16 on the way count: a program that leaves them out, or rounds other values in their place, can miss the bound.
Values may be sent and summed in bfloat16 or wider, within the bound.
A program may use at most 128 MiB of HBM per device.

v0:
```python
import jax
import jax.numpy as jnp
from jax import lax
from jax.sharding import PartitionSpec as P

HEADS = 20
HEAD = 64


def fold_keys(carry, piece, query_heads, own_start, own_count):
    top_score, total, weighted = carry
    count = piece.shape[1]
    heads = query_heads.shape[0]
    size = query_heads.shape[2]
    keys_part = piece[0].reshape(count, heads, size).transpose(1, 0, 2)
    vals_part = piece[1].reshape(count, heads, size).transpose(1, 0, 2)
    places = jnp.arange(count, dtype=jnp.int32)
    inside = (places >= own_start) & (places < own_start + own_count)

    def per_head(items):
        head_top, head_total, head_sum, head_query, head_keys, head_vals = items
        scores = jnp.dot(head_query, head_keys.T, preferred_element_type=jnp.float32)
        scores = jnp.where(inside[None, :], jnp.float32(-1e30), scores)
        new_top = jnp.maximum(head_top, scores.max(axis=-1))
        factor = jnp.exp(head_top - new_top)
        weights = jnp.exp(scores - new_top[:, None])
        upper = weights.astype(jnp.bfloat16)
        lower = (weights - upper.astype(jnp.float32)).astype(jnp.bfloat16)
        head_total = head_total * factor + weights.sum(axis=-1)
        product = jnp.dot(upper, head_vals, preferred_element_type=jnp.float32) + jnp.dot(
            lower, head_vals, preferred_element_type=jnp.float32
        )
        head_sum = head_sum * factor[:, None] + product
        return (new_top, head_total, head_sum)

    return lax.map(per_head, (top_score, total, weighted, query_heads, keys_part, vals_part))


def shards(tokens, stale_kv, stale_moments, norm_gain, norm_bias, w_query, w_key, w_value, w_out):
    band, width, chans = (tokens.shape[1], tokens.shape[2], tokens.shape[3])
    tok_count = band * width
    groups = stale_moments.shape[3]
    per_group = chans // groups
    strips = lax.axis_size("strips")
    flat = tokens.reshape(tok_count, chans).astype(jnp.float32)
    grouped = flat.reshape(tok_count, groups, per_group)
    fresh = jnp.stack([grouped.sum(axis=(0, 2)), (grouped * grouped).sum(axis=(0, 2))])
    own_moments = stale_moments[0]
    own_kv = stale_kv[0]
    totals = lax.psum(own_moments[0], "strips")
    mixed = totals - own_moments[0] + fresh
    count = float(tok_count * strips * per_group)
    mean = mixed[0] / count
    var = mixed[1] / count - mean * mean
    rstd = lax.rsqrt(var + 1e-05)
    normed = ((grouped - mean[None, :, None]) * rstd[None, :, None]).reshape(tok_count, chans)
    normed = (normed * norm_gain + norm_bias).astype(jnp.bfloat16)
    strip_index = lax.axis_index("strips")
    pieces = (
        lax.all_gather(w_query, "rows", axis=0, tiled=True),
        lax.all_gather(w_key, "rows", axis=0, tiled=True),
        lax.all_gather(w_value, "rows", axis=0, tiled=True),
    )
    columns = normed
    query_sum, key_sum, value_sum = tuple(
        (jnp.dot(columns, piece, preferred_element_type=jnp.float32) for piece in pieces)
    )
    query = (query_sum * (1.0 / HEAD**0.5)).astype(jnp.bfloat16)
    key = key_sum.astype(jnp.bfloat16)
    value = value_sum.astype(jnp.bfloat16)
    fresh_kv = jnp.stack([key, value])
    query_heads = query.reshape(tok_count, HEADS, HEAD).transpose(1, 0, 2)
    start_carry = (
        jnp.full((HEADS, tok_count), -1e30, jnp.float32),
        jnp.zeros((HEADS, tok_count), jnp.float32),
        jnp.zeros((HEADS, tok_count, HEAD), jnp.float32),
    )
    carry = fold_keys(start_carry, fresh_kv, query_heads, 0, 0)
    own_start = strip_index * tok_count
    top_score, total, weighted = fold_keys(
        carry,
        lax.all_gather(own_kv, "strips", axis=1, tiled=True),
        query_heads,
        own_start,
        tok_count,
    )
    heads_out = (
        (weighted / total[..., None])
        .transpose(1, 0, 2)
        .reshape(tok_count, HEADS * HEAD)
        .astype(jnp.bfloat16)
    )
    columns = heads_out
    attended = jnp.dot(
        columns,
        lax.all_gather(w_out, "rows", axis=0, tiled=True),
        preferred_element_type=jnp.float32,
    )
    attended = attended.astype(jnp.bfloat16)
    return (
        attended.reshape(1, band, width, chans),
        fresh_kv[None],
        fresh[0][None, None],
        fresh[1][None, None],
    )


def solution(mesh):
    in_specs = (
        P("rows", None, "strips", None),
        P("rows", None, "strips", None),
        P("rows", "strips", None, None),
        P(),
        P(),
        P("rows", None),
        P("rows", None),
        P("rows", None),
        P("rows", None),
    )
    out_specs = (
        P("rows", None, "strips", None),
        P("rows", None, "strips", None),
        P("rows", "strips", None),
        P("rows", "strips", None),
    )
    return jax.shard_map(shards, mesh=mesh, in_specs=in_specs, out_specs=out_specs, check_vma=False)
```

profile of v0, /device:TPU:16, one launch (start us, length us, event | category | flops | bytes accessed | tf_op | source)
XLA Modules:
  0.0 1437.9 jit_solution(8193434290804140495)
XLA Ops:
  10.0 4.1 copy.42
  14.8 7.1 psum.7
  23.9 292.4 %all-gather.13.cloned.1.call-done = bf16[64,20,1280]{2,1,0:T(8,128)(2,1)} async-done(((bf16[1,20,1280]{2,1,0:T(8,128)(2,1)}), bf16[64,20,1280]{2,1,0:T(8,128)(2,1)}) %all-gather.13.cloned.1.call-update) | async-done | bytes 3276816 | tf_op jit(solution)/shard_map/all_gather | solution.py:60
  316.2 4.6 reshape.127
  320.9 3.6 fusion.49
  324.5 1.6 copy.36
  327.2 291.7 %all-gather.15.cloned.1.call-done = bf16[64,20,1280]{2,1,0:T(8,128)(2,1)} async-done(((bf16[1,20,1280]{2,1,0:T(8,128)(2,1)}), bf16[64,20,1280]{2,1,0:T(8,128)(2,1)}) %all-gather.15.cloned.1.call-update) | async-done | bytes 3276816 | tf_op jit(solution)/shard_map/all_gather | solution.py:61
  618.9 6.1 reshape.129
  625.0 3.7 convolution_convert_fusion.2
  630.0 291.4 %all-gather.17.cloned.1.call-done = bf16[64,20,1280]{2,1,0:T(8,128)(2,1)} async-done(((bf16[1,20,1280]{2,1,0:T(8,128)(2,1)}), bf16[64,20,1280]{2,1,0:T(8,128)(2,1)}) %all-gather.17.cloned.1.call-update) | async-done | bytes 3276816 | tf_op jit(solution)/shard_map/all_gather | solution.py:62
  921.4 6.1 reshape.131
  927.5 4.6 convolution_convert_fusion.1
  932.1 2.2 copy.38
  934.4 2.7 maximum_bitcast_fusion
  937.0 286.7 %all-gather.19.cloned.1.call-done = bf16[64,20,1280]{2,1,0:T(8,128)(2,1)} async-done(((bf16[1,20,1280]{2,1,0:T(8,128)(2,1)}), bf16[64,20,1280]{2,1,0:T(8,128)(2,1)}) %all-gather.19.cloned.1.call-update) | async-done | bytes 3276816 | tf_op jit(solution)/shard_map/all_gather | solution.py:96
  1223.7 6.1 reshape.133
  1231.3 82.3 %while.28 = (s32[]{:T(128)}, f32[20,384]{1,0:T(8,128)S(1)}, f32[20,384]{1,0:T(8,128)S(1)}, f32[20,384,64]{1,2,0:T(8,128)}, bf16[20,384,64]{2,1,0:T(8,128)(2,1)S(...) while((s32[]{:T(128)}, f32[20,384]{1,0:T(8,128)S(1)}, ...), condition=%wide.region_8.9_spmd, body=%wide.region_5.8_spmd.sunk | while | flops 58148352 | bytes 2930277 | solution.py:36
  1233.5 1.7 fusion.90
  1237.6 1.7 fusion.90
  1241.8 1.7 fusion.90
  1245.9 1.7 fusion.90
  1250.0 1.7 fusion.90
  1254.1 1.7 fusion.90
  1258.2 1.7 fusion.90
  1262.3 1.7 fusion.90
  1266.4 1.7 fusion.90
  1270.6 1.7 fusion.90
  1274.7 1.7 fusion.90
  1278.8 1.7 fusion.90
  1282.9 1.7 fusion.90
  1287.0 1.7 fusion.90
  1291.1 1.7 fusion.90
  1295.3 1.7 fusion.90
  1299.4 1.7 fusion.90
  1303.5 1.7 fusion.90
  1307.6 1.7 fusion.90
  1311.7 1.7 fusion.90
  1313.7 6.2 fusion.58
  1320.1 106.6 %while.29 = (s32[]{:T(128)}, f32[20,384]{1,0:T(8,128)S(1)}, f32[20,384,64]{1,2,0:T(8,128)S(1)}, f32[20,384]{1,0:T(8,128)S(1)}, f32[20,384]{1,0:T(8,128)S(1)}, /*...) while((s32[]{:T(128)}, f32[20,384]{1,0:T(8,128)S(1)}, ...), condition=%wide.region_12.13_spmd.clone, body=%wide.region_9.12_spmd.clone.sunk | while | flops 233060352 | bytes 10554513 | solution.py:36
  1323.3 1.6 fusion.100
  1327.0 1.5 fusion.99
  1328.6 1.6 fusion.100
  1332.4 1.5 fusion.99
  1333.9 1.6 fusion.100
  1339.2 1.6 fusion.100
  1343.0 1.5 fusion.99
  1344.6 1.6 fusion.100
  1348.4 1.5 fusion.99
  1349.9 1.6 fusion.100
  1355.2 1.6 fusion.100
  1360.6 1.6 fusion.100
  1365.9 1.6 fusion.100
  1371.2 1.6 fusion.100
  1376.6 1.6 fusion.100
  1381.9 1.6 fusion.100
  1387.2 1.6 fusion.100
  1392.5 1.6 fusion.100
  1397.9 1.6 fusion.100
  1403.2 1.6 fusion.100
  1408.5 1.6 fusion.100
  1413.9 1.6 fusion.100
  1419.2 1.6 fusion.100
  1424.5 1.6 fusion.100
  1427.0 4.4 convolution_convert_fusion
  (362 shorter events, 123.9 us)
Async XLA Ops:
  7.2 309.1 %all-gather.13.cloned.1.call-start = ((), (), s32[]{:S(2)}) async-start(), calls=%async_computation.1 | async-start | bytes 3993600 | tf_op jit(solution)/shard_map/all_gather | solution.py:60
  7.9 611.0 %all-gather.15.cloned.1.call-start = ((), (), s32[]{:S(2)}) async-start(), calls=%async_computation.2 | async-start | bytes 3993600 | tf_op jit(solution)/shard_map/all_gather | solution.py:61
  8.6 912.7 %all-gather.17.cloned.1.call-start = ((), (), s32[]{:S(2)}) async-start(), calls=%async_computation.3 | async-start | bytes 3993600 | tf_op jit(solution)/shard_map/all_gather | solution.py:62
  9.4 1214.3 %all-gather.19.cloned.1.call-start = ((), (), s32[]{:S(2)}) async-start(), calls=%async_computation.4 | async-start | bytes 3993600 | tf_op jit(solution)/shard_map/all_gather | solution.py:96
  10.0 4.2 copy-start.1
  10.0 1303.7 %all-gather.11.cloned.1.call-start = ((), (), s32[]{:S(2)}) async-start(), calls=%async_computation | async-start | bytes 9830400 | tf_op jit(solution)/shard_map/all_gather | solution.py:82
  14.1 0.7 copy-start.4
  14.1 8.4 copy-start.2
  14.1 8.4 copy-start.3
  22.0 298.8 %copy-start.5 = (f32[32]{0:T(128)}, f32[32]{0:T(128)S(1)}, u32[]{:S(2)}) copy-start(f32[32]{0:T(128)S(1)} %reduce_sum.58) | copy-start | bytes 388
  22.2 298.7 %copy-start.6 = (f32[32]{0:T(128)}, f32[32]{0:T(128)S(1)}, u32[]{:S(2)}) copy-start(f32[32]{0:T(128)S(1)} %reduce_sum.61) | copy-start | bytes 388
  1313.7 6.2 copy-start
Sparse Core Ops, SparseCore 0:
  9.8 306.3 all-gather.12
  318.0 300.8 all-gather.14
  620.7 300.6 all-gather.16
  923.0 300.6 all-gather.18
  1225.4 56.4 all-gather.10
where the time goes:
time: 1440 us
  waiting for transfers between devices  1160 us (81%)
  matrix products  186 us (13%)
  local copies, waits for them, and re-layouts  45.6 us (3%)
  other arithmetic  17.7 us (1%)
    all_gather x1, waiting for transfers between devices, shards(): lax.all_gather(w_query, 'rows', axis=0, tiled=True)  292 us
    all_gather x1, waiting for transfers between devices, shards(): lax.all_gather(w_key, 'rows', axis=0, tiled=True)  292 us
    all_gather x1, waiting for transfers between devices, shards(): lax.all_gather(w_value, 'rows', axis=0, tiled=True)  291 us
    all_gather x1, waiting for transfers between devices, shards(): lax.all_gather(w_out, 'rows', axis=0, tiled=True)  287 us
    dot_general x40, matrix products, per_head(): jnp.dot(lower, head_vals, preferred_element_type=jnp.float32)  66.5 us
    dot_general x40, matrix products, per_head(): jnp.dot(head_query, head_keys.T, preferred_element_type=jnp.float32)  52.2 us
    dot_general x40, matrix products, per_head(): jnp.dot(upper, head_vals, preferred_element_type=jnp.float32)  51.5 us
  transfers between devices with their start and end apart: 5, of which 4 were waited for; matrix products, arithmetic and copies ran while one was open for 9% of the time, Pallas kernels for 0%

commit v1 on v0

v1 whole, which is shorter than its diff:
```python
import jax
import jax.numpy as jnp
from jax import lax
from jax.experimental import pallas as pl
from jax.experimental.pallas import tpu as pltpu
from jax.sharding import PartitionSpec as P

MESH = pl.DeviceIdType.MESH
F32 = jnp.float32
BF16 = jnp.bfloat16

TOK = 384
CH = 1280
HALF = 640
LANES = 128
WAVES = 5
NX, NZ, NY = 4, 8, 2
SHARD = 20
GROUPS = 32
PER_GROUP = 40


def dot(a, b, dims=((1,), (0,)), precision=None):
    return lax.dot_general(a, b, (dims, ((), ())), precision=precision, preferred_element_type=F32)


def kernel(
    tok_ref, kv_ref, mom_ref, gain_ref, bias_ref, wq_ref, wk_ref, wv_ref, wo_ref,
    att_ref, fkv_ref, fs_ref, fq_ref,
    w_buf, wo_buf, w_nat, wo_nat, pick_a, pick_b, tail, kvb, nrm, qb, ho, ho_out, moms,
    y_s, y_r, z_s, z_r, x_s, x_r, xx_s, xx_r, zo_s, zo_r, xo_s, xo_r, xxo_s, xxo_r,
    kv_s, kv_r, kv_l, mom_s, mom_r, nrm_s, nrm_r, fkv_s, fkv_r, fkv_l, ho_s, ho_r, won_s, won_r,
):
    row = lax.axis_index("rows")
    strip = lax.axis_index("strips")
    ylo = row % 2
    z = (row // 2) % NZ
    x = row // (2 * NZ)
    core = strip % 2
    yhi = strip // 2

    sib = (row, yhi * 2 + 1 - core)
    far = (row, (1 - yhi) * 2 + core)
    far_other = (row, (1 - yhi) * 2 + 1 - core)
    y_peer = (x * 16 + z * 2 + 1 - ylo, strip)
    z_peers = [(x * 16 + ((z + d) % NZ) * 2 + ylo, strip) for d in range(1, NZ)]
    xl = (x + NX - 1) % NX
    xr = (x + 1) % NX
    x_far = (x + 2) % NX
    x_left = (xl * 16 + z * 2 + ylo, strip)
    x_right = (xr * 16 + z * 2 + ylo, strip)

    barrier = pltpu.get_barrier_semaphore()
    everyone = [sib, far, far_other, y_peer, x_left, x_right] + z_peers
    for peer in everyone:
        pl.semaphore_signal(barrier, inc=1, device_id=peer, device_id_type=MESH)

    def remote(src, dst, send, recv, to):
        return pltpu.make_async_remote_copy(
            src_ref=src, dst_ref=dst, send_sem=send, recv_sem=recv, device_id=to, device_id_type=MESH
        )

    mine = pl.ds(pl.multiple_of(core * HALF, LANES), HALF)
    for t, ref in enumerate((wq_ref, wk_ref, wv_ref, wo_ref)):
        rows = ref[:, mine]
        for g in range(WAVES):
            piece = rows[:16, g * LANES : (g + 1) * LANES]
            if t < 3:
                w_buf[g, x, z, ylo, t] = piece
            else:
                wo_buf[x, z, ylo, g] = piece
        tail[4 * t : 4 * t + 4, :] = rows.astype(F32)[16:SHARD, :]
    rest = tail[...].astype(BF16)
    for g in range(WAVES):
        w_buf[g, x, z, ylo, 3] = rest[:, g * LANES : (g + 1) * LANES]
    moms[0] = jnp.zeros((8, LANES), F32)
    moms[0, 0:2, 0:GROUPS] = mom_ref[...]

    pl.semaphore_wait(barrier, len(everyone))

    def y_copies():
        here = w_buf.at[:, x, z, ylo]
        ohere = wo_buf.at[x, z, ylo]
        return [
            remote(here, here, y_s.at[0], y_r.at[0], y_peer),
            remote(ohere, ohere, y_s.at[1], y_r.at[1], y_peer),
        ]

    def y_wait():
        there = w_buf.at[:, x, z, 1 - ylo]
        othere = wo_buf.at[x, z, 1 - ylo]
        remote(there, there, y_s.at[0], y_r.at[0], y_peer).wait_recv()
        remote(othere, othere, y_s.at[1], y_r.at[1], y_peer).wait_recv()

    def z_copies(g):
        return [
            remote(w_buf.at[g, x, z], w_buf.at[g, x, z], z_s.at[g, d], z_r.at[g, d], z_peers[d])
            for d in range(NZ - 1)
        ]

    def z_wait(g):
        for d in range(NZ - 1):
            there = w_buf.at[g, x, (z + NZ - 1 - d) % NZ]
            remote(there, there, z_s.at[g, d], z_r.at[g, d], z_peers[d]).wait_recv()

    def zo_copies():
        return [
            remote(wo_buf.at[x, z], wo_buf.at[x, z], zo_s.at[d], zo_r.at[d], z_peers[d])
            for d in range(NZ - 1)
        ]

    def zo_wait():
        for d in range(NZ - 1):
            there = wo_buf.at[x, (z + NZ - 1 - d) % NZ]
            remote(there, there, zo_s.at[d], zo_r.at[d], z_peers[d]).wait_recv()

    def x_copies(buf, send, recv):
        here = buf(x, 0, NZ)
        return [
            remote(here, here, send(0), recv(0), x_right),
            remote(here, here, send(1), recv(1), x_left),
        ]

    def x_wait(buf, send, recv):
        for i, at in ((0, xl), (1, xr)):
            there = buf(at, 0, NZ)
            remote(there, there, send(i), recv(i), x_right).wait_recv()

    def xx_copies(buf, send, recv):
        first, second = buf(xl, 0, NZ // 2), buf(xr, NZ // 2, NZ // 2)
        return [
            remote(first, first, send(0), recv(0), x_right),
            remote(second, second, send(1), recv(1), x_left),
        ]

    def xx_wait(buf, send, recv):
        for i in (0, 1):
            there = buf(x_far, i * (NZ // 2), NZ // 2)
            remote(there, there, send(i), recv(i), x_right).wait_recv()

    def wave(g, send, recv):
        return (
            lambda at, first, count: w_buf.at[g, at, pl.ds(first, count)],
            lambda i: send.at[g, i],
            lambda i: recv.at[g, i],
        )

    def owave(send, recv):
        return (
            lambda at, first, count: wo_buf.at[at, pl.ds(first, count)],
            lambda i: send.at[i],
            lambda i: recv.at[i],
        )

    def lanes(which, g):
        return pl.ds(pl.multiple_of(which * HALF + g * LANES, LANES), LANES)

    def block(i):
        return pl.ds(i * TOK, TOK)

    def kv_copies(g):
        mine_g, other_g = kv_ref.at[:, :, lanes(core, g)], kv_ref.at[:, :, lanes(1 - core, g)]
        return [
            remote(other_g, kvb.at[g, :, block(0)], kv_s.at[g, 0], kv_r.at[g, 0], sib),
            remote(mine_g, kvb.at[g, :, block(2)], kv_s.at[g, 1], kv_r.at[g, 1], far),
            remote(other_g, kvb.at[g, :, block(3)], kv_s.at[g, 2], kv_r.at[g, 2], far_other),
        ]

    def kv_own(g):
        return pltpu.make_async_copy(kv_ref.at[:, :, lanes(core, g)], kvb.at[g, :, block(5)], kv_l.at[g])

    def kv_wait(g):
        for i, b in enumerate((0, 2, 3)):
            there = kvb.at[g, :, block(b)]
            remote(there, there, kv_s.at[g, i], kv_r.at[g, i], sib).wait_recv()
        kv_own(g).wait()

    def mom_copies():
        return [
            remote(moms.at[0], moms.at[i + 1], mom_s.at[i], mom_r.at[i], to)
            for i, to in enumerate((sib, far, far_other))
        ]

    def nrm_copy():
        return remote(nrm.at[pl.ds(0, TOK)], nrm.at[pl.ds(TOK, TOK)], nrm_s, nrm_r, sib)

    def fkv_copy(g):
        return remote(kvb.at[g, :, block(4)], fkv_ref.at[:, :, lanes(core, g)], fkv_s.at[g], fkv_r.at[g], sib)

    def fkv_own(g):
        return pltpu.make_async_copy(kvb.at[g, :, block(1)], fkv_ref.at[:, :, lanes(core, g)], fkv_l.at[g])

    def fkv_wait(g):
        there = fkv_ref.at[:, :, lanes(1 - core, g)]
        remote(there, there, fkv_s.at[g], fkv_r.at[g], sib).wait_recv()

    def ho_copy(g):
        return remote(ho_out.at[g], ho.at[core * WAVES + g], ho_s.at[g], ho_r.at[g], sib)

    def ho_wait(g):
        there = ho.at[(1 - core) * WAVES + g]
        remote(there, there, ho_s.at[g], ho_r.at[g], sib).wait_recv()

    def won_copy():
        return remote(wo_nat.at[core], wo_nat.at[core], won_s, won_r, sib)

    def start(copies):
        for copy in copies:
            copy.start()

    start(mom_copies())
    start(y_copies())
    start(kv_copies(0))
    kv_own(0).start()
    start(kv_copies(1))
    kv_own(1).start()

    channel = lax.broadcasted_iota(jnp.int32, (CH, LANES), 0)
    group = lax.broadcasted_iota(jnp.int32, (CH, LANES), 1)
    member = jnp.where((channel >= group * PER_GROUP) & (channel < (group + 1) * PER_GROUP), 1.0, 0.0)
    toks = tok_ref[...].astype(F32)
    sums = jnp.sum(toks, axis=0, keepdims=True)
    squares = jnp.sum(toks * toks, axis=0, keepdims=True)
    pick = lax.broadcasted_iota(jnp.int32, (8, CH), 0)
    stacked = jnp.where(pick == 0, sums, jnp.where(pick == 1, squares, 0.0))
    fresh = dot(stacked, member, precision=lax.Precision.HIGHEST)
    fs_ref[...] = fresh[0:1, 0:GROUPS]
    fq_ref[...] = fresh[1:2, 0:GROUPS]

    y_wait()
    start(z_copies(0))
    start(z_copies(1))

    k_at = lax.broadcasted_iota(jnp.int32, (320, 256), 0)
    j_at = lax.broadcasted_iota(jnp.int32, (320, 256), 1)
    base = (j_at >> 4) * SHARD
    pick_a[...] = jnp.where(k_at == base + (j_at & 15), 1.0, 0.0).astype(BF16)
    for t in range(4):
        hit = (k_at == base + 16 + (j_at & 3)) & (((j_at >> 2) & 3) == t)
        pick_b[t] = jnp.where(hit, 1.0, 0.0).astype(BF16)

    for i in range(3):
        there = moms.at[i + 1]
        remote(there, there, mom_s.at[i], mom_r.at[i], sib).wait_recv()
    mixed = (moms[1] + moms[2] + moms[3]) + fresh
    count = float(TOK * 4 * PER_GROUP)
    mean = mixed[0:1, :] / count
    var = mixed[1:2, :] / count - mean * mean
    rstd = lax.rsqrt(var + 1e-05)
    pick = lax.broadcasted_iota(jnp.int32, (8, LANES), 0)
    inside = lax.broadcasted_iota(jnp.int32, (8, LANES), 1) < GROUPS
    stats = jnp.where(inside, jnp.where(pick == 0, mean, jnp.where(pick == 1, rstd, 0.0)), 0.0)
    spread = dot(stats, member, dims=((1,), (1,)), precision=lax.Precision.HIGHEST)
    normed = (tok_ref[...].astype(F32) - spread[0:1, :]) * spread[1:2, :]
    nrm[0:TOK, :] = (normed * gain_ref[...] + bias_ref[...]).astype(BF16)
    nrm_copy().start()

    z_wait(0)
    start(x_copies(*wave(0, x_s, x_r)))
    there = nrm.at[pl.ds(TOK, TOK)]
    remote(there, there, nrm_s, nrm_r, sib).wait_recv()

    low = lax.broadcasted_iota(jnp.int32, (TOK, LANES), 1) < LANES // 2

    def attend(g, which):
        query = qb[pl.ds(which * TOK, TOK), :]
        keys = kvb[g, 0, pl.ds(which * 2 * TOK, 4 * TOK), :]
        values = kvb[g, 1, pl.ds(which * 2 * TOK, 4 * TOK), :]
        values = jnp.concatenate([values, jnp.ones_like(values)], axis=1)
        results = []
        for head in range(2):
            own = jnp.where(low if head == 0 else ~low, query, jnp.zeros_like(query))
            scores = dot(own, keys, dims=((1,), (1,)))
            top = jnp.max(scores, axis=1, keepdims=True)
            weights = jnp.exp(scores - top).astype(BF16)
            both = dot(weights, values)
            results.append(both[:, :LANES] / both[:, LANES:])
        return jnp.where(low, results[0], results[1]).astype(BF16)

    def step(g, carry):
        @pl.when(g + 2 < WAVES)
        def _():
            start(z_copies(g + 2))
            start(kv_copies(g + 2))
            kv_own(g + 2).start()

        @pl.when(g == 1)
        def _():
            start(zo_copies())

        @pl.when(g + 1 < WAVES)
        def _():
            z_wait(g + 1)
            start(x_copies(*wave(g + 1, x_s, x_r)))

        @pl.when(g == 2)
        def _():
            zo_wait()
            start(x_copies(*owave(xo_s, xo_r)))

        x_wait(*wave(g, x_s, x_r))
        start(xx_copies(*wave(g, xx_s, xx_r)))

        @pl.when(g == 3)
        def _():
            x_wait(*owave(xo_s, xo_r))
            start(xx_copies(*owave(xxo_s, xxo_r)))

        xx_wait(*wave(g, xx_s, xx_r))

        for at in range(NX):
            heads = jnp.concatenate([w_buf[g, at, :, :, t].reshape(256, LANES) for t in range(3)], axis=1)
            part = dot(pick_a[...], heads)
            rest = w_buf[g, at, :, :, 3].reshape(256, LANES)
            for t in range(3):
                both = part[:, t * LANES : (t + 1) * LANES] + dot(pick_b[t], rest)
                w_nat[at * 320 : (at + 1) * 320, t * LANES : (t + 1) * LANES] = both.astype(BF16)
        result = dot(nrm[...], w_nat[...])
        qb[...] = (result[:, :LANES] * 0.125).astype(BF16)
        for t in range(2):
            new = result[:, (t + 1) * LANES : (t + 2) * LANES].astype(BF16)
            kvb[g, t, block(1)] = new[:TOK]
            kvb[g, t, block(4)] = new[TOK:]
        fkv_own(g).start()
        fkv_copy(g).start()
        kv_wait(g)

        ho_out[g] = attend(g, 1)
        ho_copy(g).start()
        ho[core * WAVES + g] = attend(g, 0)
        return carry

    lax.fori_loop(0, WAVES, step, 0)

    xx_wait(*owave(xxo_s, xxo_r))
    for at in range(NX):
        for g in range(WAVES):
            part = dot(pick_a[...], wo_buf[at, :, :, g].reshape(256, LANES))
            part = part + dot(pick_b[3], w_buf[g, at, :, :, 3].reshape(256, LANES))
            wo_nat[core, at * 320 : (at + 1) * 320, g * LANES : (g + 1) * LANES] = part.astype(BF16)
    won_copy().start()
    for g in range(WAVES):
        ho_wait(g)
    there = wo_nat.at[1 - core]
    remote(there, there, won_s, won_r, sib).wait_recv()
    lhs = jnp.concatenate([ho[i] for i in range(2 * WAVES)], axis=1)
    for i in range(2):
        att_ref[:, i * HALF : (i + 1) * HALF] = dot(lhs, wo_nat[i]).astype(BF16)

    for copy in mom_copies() + y_copies() + zo_copies() + [nrm_copy(), won_copy()]:
        copy.wait_send()
    for copy in x_copies(*owave(xo_s, xo_r)) + xx_copies(*owave(xxo_s, xxo_r)):
        copy.wait_send()

    def drain(g, carry):
        for copy in z_copies(g) + kv_copies(g) + [fkv_copy(g), ho_copy(g)]:
            copy.wait_send()
        for copy in x_copies(*wave(g, x_s, x_r)) + xx_copies(*wave(g, xx_s, xx_r)):
            copy.wait_send()
        fkv_wait(g)
        fkv_own(g).wait()
        return carry

    lax.fori_loop(0, WAVES, drain, 0)


def shards(tokens, stale_kv, stale_moments, norm_gain, norm_bias, w_query, w_key, w_value, w_out):
    vmem = pl.BlockSpec(memory_space=pltpu.VMEM)
    hbm = pl.BlockSpec(memory_space=pl.ANY)
    dma = pltpu.SemaphoreType.DMA
    z1 = NZ - 1
    attended, fresh_kv, sums, squares = pl.pallas_call(
        kernel,
        out_shape=(
            jax.ShapeDtypeStruct((TOK, CH), BF16),
            jax.ShapeDtypeStruct((2, TOK, CH), BF16),
            jax.ShapeDtypeStruct((1, GROUPS), F32),
            jax.ShapeDtypeStruct((1, GROUPS), F32),
        ),
        in_specs=[vmem, hbm] + [vmem] * 7,
        out_specs=(vmem, hbm, vmem, vmem),
        scratch_shapes=[
            pltpu.VMEM((WAVES, NX, NZ, NY, 4, 16, LANES), BF16),
            pltpu.VMEM((NX, NZ, NY, WAVES, 16, LANES), BF16),
            pltpu.VMEM((CH, 3 * LANES), BF16),
            pltpu.VMEM((2, CH, HALF), BF16),
            pltpu.VMEM((320, 256), BF16),
            pltpu.VMEM((4, 320, 256), BF16),
            pltpu.VMEM((16, HALF), F32),
            pltpu.VMEM((WAVES, 2, 6 * TOK, LANES), BF16),
            pltpu.VMEM((2 * TOK, CH), BF16),
            pltpu.VMEM((2 * TOK, LANES), BF16),
            pltpu.VMEM((2 * WAVES, TOK, LANES), BF16),
            pltpu.VMEM((WAVES, TOK, LANES), BF16),
            pltpu.VMEM((4, 8, LANES), F32),
            dma((2,)), dma((2,)),
            dma((WAVES, z1)), dma((WAVES, z1)),
            dma((WAVES, 2)), dma((WAVES, 2)),
            dma((WAVES, 2)), dma((WAVES, 2)),
            dma((z1,)), dma((z1,)),
            dma((2,)), dma((2,)),
            dma((2,)), dma((2,)),
            dma((WAVES, 3)), dma((WAVES, 3)), dma((WAVES,)),
            dma((3,)), dma((3,)),
            dma, dma,
            dma((WAVES,)), dma((WAVES,)), dma((WAVES,)),
            dma((WAVES,)), dma((WAVES,)),
            dma, dma,
        ],
        compiler_params=pltpu.CompilerParams(
            collective_id=0, has_side_effects=True, vmem_limit_bytes=60 << 20
        ),
        name="block",
    )(
        tokens.reshape(TOK, CH), stale_kv[0], stale_moments[0, 0],
        norm_gain[None], norm_bias[None], w_query, w_key, w_value, w_out,
    )
    return (
        attended.reshape(tokens.shape),
        fresh_kv[None],
        sums[None],
        squares[None],
    )


def solution(mesh):
    in_specs = (
        P("rows", None, "strips", None),
        P("rows", None, "strips", None),
        P("rows", "strips", None, None),
        P(),
        P(),
        P("rows", None),
        P("rows", None),
        P("rows", None),
        P("rows", None),
    )
    out_specs = (
        P("rows", None, "strips", None),
        P("rows", None, "strips", None),
        P("rows", "strips", None),
        P("rows", "strips", None),
    )
    return jax.shard_map(shards, mesh=mesh, in_specs=in_specs, out_specs=out_specs, check_vma=False)
```

time: 1440 us -> 126 us (0.09)
  the two profiles are of different devices: /device:TPU:16 before, /device:TPU:1 now
where the time goes in v1:
time: 126 us; the launch traced here: 124 us
  Pallas kernels  116 us (92%)
  local copies, waits for them, and re-layouts  7.24 us (6%)
    pallas_call x1, Pallas kernels, shards(): pl.pallas_call(kernel, out_shape=(jax.ShapeDtypeStruct((TOK, CH), BF16),...  116 us
    unnamed x10, local copies, waits for them, and re-layouts  4.65 us

profile of v1, /device:TPU:1, one launch (start us, length us, event | category | flops | bytes accessed | tf_op | source)
XLA Modules:
  0.0 124.4 jit_solution(13924373538104726723)
XLA Ops:
  0.6 1.3 %broadcast_in_dim.15.gain_ref = f32[1,1280]{1,0:T(1,128)} reshape(f32[1280]{0:T(1024)} %param.12) | data formatting | bytes 10240 | tf_op jit(solution)/shard_map/broadcast_in_dim | solution.py:416
  1.9 1.3 %broadcast_in_dim.16.bias_ref = f32[1,1280]{1,0:T(1,128)} reshape(f32[1280]{0:T(1024)} %param.13) | data formatting | bytes 10240 | tf_op jit(solution)/shard_map/broadcast_in_dim | solution.py:416
  3.2 116.5 %block.1 = (bf16[384,1280]{1,0:T(8,128)(2,1)}, bf16[2,384,1280]{2,1,0:T(8,128)(2,1)}, f32[1,32]{1,0:T(1,128)}, f32[1,32]{1,0:T(1,128)}) custom-call(bf16[384,1280]{1,0:T(8,128)(2,1)} %bitcast.9, bf16[2,384,1280]{2,1,0:T(8,128)(2,1)} %bitcast.7, f32[2,32]{1,0:T(2,128)} %bitcast.11, f32[1,1280]{1,0:T(1,128)} %broadcast_in_dim.15.gain_ref, ...), custom_call_target="tpu_custom_call" | custom-call | tf_op jit(solution)/shard_map/block/pallas_call | solution.py:372
  119.7 0.0 copy-start
  119.7 2.4 %copy.17 = bf16[1,24,16,1280]{3,2,1,0:T(8,128)(2,1)} copy(bf16[1,24,16,1280]{3,2,1,0:T(8,128)(2,1)} %bitcast.10) | data formatting | bytes 1966080
  122.1 0.0 copy-done
  122.1 0.0 copy-start.2
  122.1 0.0 copy-start.1
  122.1 1.3 %copy.18 = bf16[1,2,384,1280]{3,2,1,0:T(8,128)(2,1)} copy(bf16[1,2,384,1280]{3,2,1,0:T(8,128)(2,1)S(1)} %bitcast.8) | data formatting | bytes 3932160
  123.4 0.0 copy-done.2
  123.4 0.5 copy.19
  123.9 0.0 copy-done.1
  123.9 0.5 copy.20
Async XLA Ops:
  119.7 2.4 %copy-start = (bf16[2,384,1280]{2,1,0:T(8,128)(2,1)S(1)}, bf16[2,384,1280]{2,1,0:T(8,128)(2,1)}, u32[]{:S(2)}) copy-start(bf16[2,384,1280]{2,1,0:T(8,128)(2,1)} %get-tuple-element.9) | copy-start | bytes 5898244
  122.1 1.3 %copy-start.2 = (f32[1,32]{1,0:T(1,128)S(1)}, f32[1,32]{1,0:T(1,128)}, u32[]{:S(2)}) copy-start(f32[1,32]{1,0:T(1,128)} %get-tuple-element.10) | copy-start | bytes 388
  122.1 1.8 %copy-start.1 = (f32[1,32]{1,0:T(1,128)S(1)}, f32[1,32]{1,0:T(1,128)}, u32[]{:S(2)}) copy-start(f32[1,32]{1,0:T(1,128)} %get-tuple-element.11) | copy-start | bytes 388

commit v2 on v1

--- a/solution.py
+++ b/solution.py
@@ -28,7 +28,7 @@
     tok_ref, kv_ref, mom_ref, gain_ref, bias_ref, wq_ref, wk_ref, wv_ref, wo_ref,
     att_ref, fkv_ref, fs_ref, fq_ref,
     w_buf, wo_buf, w_nat, wo_nat, pick_a, pick_b, tail, kvb, nrm, qb, ho, ho_out, moms,
-    y_s, y_r, z_s, z_r, x_s, x_r, xx_s, xx_r, zo_s, zo_r, xo_s, xo_r, xxo_s, xxo_r,
+    y_s, y_r, z_s, z_r, x_s, x_r, xx_s, xx_r, ox_s, ox_r, oz_s, oz_r,
     kv_s, kv_r, kv_l, mom_s, mom_r, nrm_s, nrm_r, fkv_s, fkv_r, fkv_l, ho_s, ho_r, won_s, won_r,
 ):
     row = lax.axis_index("rows")
@@ -49,9 +49,10 @@
     x_far = (x + 2) % NX
     x_left = (xl * 16 + z * 2 + ylo, strip)
     x_right = (xr * 16 + z * 2 + ylo, strip)
+    x_across = (x_far * 16 + z * 2 + ylo, strip)
 
     barrier = pltpu.get_barrier_semaphore()
-    everyone = [sib, far, far_other, y_peer, x_left, x_right] + z_peers
+    everyone = [sib, far, far_other, y_peer, x_left, x_right, x_across] + z_peers
     for peer in everyone:
         pl.semaphore_signal(barrier, inc=1, device_id=peer, device_id_type=MESH)
 
@@ -68,7 +69,7 @@
             if t < 3:
                 w_buf[g, x, z, ylo, t] = piece
             else:
-                wo_buf[x, z, ylo, g] = piece
+                wo_buf[z, x, ylo, g] = piece
         tail[4 * t : 4 * t + 4, :] = rows.astype(F32)[16:SHARD, :]
     rest = tail[...].astype(BF16)
     for g in range(WAVES):
@@ -80,7 +81,7 @@
 
     def y_copies():
         here = w_buf.at[:, x, z, ylo]
-        ohere = wo_buf.at[x, z, ylo]
+        ohere = wo_buf.at[z, x, ylo]
         return [
             remote(here, here, y_s.at[0], y_r.at[0], y_peer),
             remote(ohere, ohere, y_s.at[1], y_r.at[1], y_peer),
@@ -88,7 +89,7 @@
 
     def y_wait():
         there = w_buf.at[:, x, z, 1 - ylo]
-        othere = wo_buf.at[x, z, 1 - ylo]
+        othere = wo_buf.at[z, x, 1 - ylo]
         remote(there, there, y_s.at[0], y_r.at[0], y_peer).wait_recv()
         remote(othere, othere, y_s.at[1], y_r.at[1], y_peer).wait_recv()
 
@@ -103,54 +104,65 @@
             there = w_buf.at[g, x, (z + NZ - 1 - d) % NZ]
             remote(there, there, z_s.at[g, d], z_r.at[g, d], z_peers[d]).wait_recv()
 
-    def zo_copies():
-        return [
-            remote(wo_buf.at[x, z], wo_buf.at[x, z], zo_s.at[d], zo_r.at[d], z_peers[d])
-            for d in range(NZ - 1)
-        ]
-
-    def zo_wait():
-        for d in range(NZ - 1):
-            there = wo_buf.at[x, (z + NZ - 1 - d) % NZ]
-            remote(there, there, zo_s.at[d], zo_r.at[d], z_peers[d]).wait_recv()
-
-    def x_copies(buf, send, recv):
-        here = buf(x, 0, NZ)
-        return [
-            remote(here, here, send(0), recv(0), x_right),
-            remote(here, here, send(1), recv(1), x_left),
-        ]
-
-    def x_wait(buf, send, recv):
+    def ox_copies():
+        here = wo_buf.at[z, x]
+        return [
+            remote(here, here, ox_s.at[i], ox_r.at[i], to) for i, to in enumerate((x_right, x_across, x_left))
+        ]
+
+    def ox_wait():
+        for i, at in enumerate((xl, x_far, xr)):
+            there = wo_buf.at[z, at]
+            remote(there, there, ox_s.at[i], ox_r.at[i], x_right).wait_recv()
+
+    def z_at(d):
+        return (z + NZ + d) % NZ
+
+    def z_peer(d):
+        return z_peers[(d - 1) % NZ]
+
+    def oz_copies():
+        here = wo_buf.at[z]
+        return [remote(here, here, oz_s.at[i], oz_r.at[i], z_peer(d)) for i, d in enumerate((1, -1, 2, -2))]
+
+    def ozz_copies():
+        left, right = wo_buf.at[z_at(-2)], wo_buf.at[z_at(2)]
+        left_half, right_half = wo_buf.at[z_at(-2), pl.ds(0, 2)], wo_buf.at[z_at(2), pl.ds(2, 2)]
+        return [
+            remote(ref, ref, oz_s.at[i + 4], oz_r.at[i + 4], z_peer(d))
+            for i, (ref, d) in enumerate(((left, 1), (right, -1), (left_half, 2), (right_half, -2)))
+        ]
+
+    def oz_wait(which):
+        for i in which:
+            there = wo_buf.at[z_at((-1, 1, -2, 2, -3, 3, 4, 4)[i])]
+            if i >= 6:
+                there = wo_buf.at[z_at(4), pl.ds(2 * (i - 6), 2)]
+            remote(there, there, oz_s.at[i], oz_r.at[i], x_right).wait_recv()
+
+    def x_copies(g):
+        here = w_buf.at[g, x]
+        return [
+            remote(here, here, x_s.at[g, 0], x_r.at[g, 0], x_right),
+            remote(here, here, x_s.at[g, 1], x_r.at[g, 1], x_left),
+        ]
+
+    def x_wait(g):
         for i, at in ((0, xl), (1, xr)):
-            there = buf(at, 0, NZ)
-            remote(there, there, send(i), recv(i), x_right).wait_recv()
-
-    def xx_copies(buf, send, recv):
-        first, second = buf(xl, 0, NZ // 2), buf(xr, NZ // 2, NZ // 2)
-        return [
-            remote(first, first, send(0), recv(0), x_right),
-            remote(second, second, send(1), recv(1), x_left),
-        ]
-
-    def xx_wait(buf, send, recv):
+            there = w_buf.at[g, at]
+            remote(there, there, x_s.at[g, i], x_r.at[g, i], x_right).wait_recv()
+
+    def xx_copies(g):
+        first, second = w_buf.at[g, xl, pl.ds(0, NZ // 2)], w_buf.at[g, xr, pl.ds(NZ // 2, NZ // 2)]
+        return [
+            remote(first, first, xx_s.at[g, 0], xx_r.at[g, 0], x_right),
+            remote(second, second, xx_s.at[g, 1], xx_r.at[g, 1], x_left),
+        ]
+
+    def xx_wait(g):
         for i in (0, 1):
-            there = buf(x_far, i * (NZ // 2), NZ // 2)
-            remote(there, there, send(i), recv(i), x_right).wait_recv()
-
-    def wave(g, send, recv):
-        return (
-            lambda at, first, count: w_buf.at[g, at, pl.ds(first, count)],
-            lambda i: send.at[g, i],
-            lambda i: recv.at[g, i],
-        )
-
-    def owave(send, recv):
-        return (
-            lambda at, first, count: wo_buf.at[at, pl.ds(first, count)],
-            lambda i: send.at[i],
-            lambda i: recv.at[i],
-        )
+            there = w_buf.at[g, x_far, pl.ds(i * (NZ // 2), NZ // 2)]
+            remote(there, there, xx_s.at[g, i], xx_r.at[g, i], x_right).wait_recv()
 
     def lanes(which, g):
         return pl.ds(pl.multiple_of(which * HALF + g * LANES, LANES), LANES)
@@ -208,12 +220,13 @@
         for copy in copies:
             copy.start()
 
+    def kv_start(g):
+        start(kv_copies(g))
+        kv_own(g).start()
+
+    start(y_copies())
     start(mom_copies())
-    start(y_copies())
-    start(kv_copies(0))
-    kv_own(0).start()
-    start(kv_copies(1))
-    kv_own(1).start()
+    kv_start(0)
 
     channel = lax.broadcasted_iota(jnp.int32, (CH, LANES), 0)
     group = lax.broadcasted_iota(jnp.int32, (CH, LANES), 1)
@@ -229,6 +242,9 @@
 
     y_wait()
     start(z_copies(0))
+    start(ox_copies())
+    kv_start(1)
+    kv_start(2)
     start(z_copies(1))
 
     k_at = lax.broadcasted_iota(jnp.int32, (320, 256), 0)
@@ -252,11 +268,16 @@
     stats = jnp.where(inside, jnp.where(pick == 0, mean, jnp.where(pick == 1, rstd, 0.0)), 0.0)
     spread = dot(stats, member, dims=((1,), (1,)), precision=lax.Precision.HIGHEST)
     normed = (tok_ref[...].astype(F32) - spread[0:1, :]) * spread[1:2, :]
-    nrm[0:TOK, :] = (normed * gain_ref[...] + bias_ref[...]).astype(BF16)
+    nrm[0:TOK, :] = (normed * gain_ref[...][None] + bias_ref[...][None]).astype(BF16)
     nrm_copy().start()
 
     z_wait(0)
-    start(x_copies(*wave(0, x_s, x_r)))
+    start(x_copies(0))
+    start(z_copies(2))
+    z_wait(1)
+    start(x_copies(1))
+    x_wait(0)
+    start(xx_copies(0))
     there = nrm.at[pl.ds(TOK, TOK)]
     remote(there, there, nrm_s, nrm_r, sib).wait_recv()
 
@@ -278,35 +299,32 @@
         return jnp.where(low, results[0], results[1]).astype(BF16)
 
     def step(g, carry):
+        @pl.when(g + 3 < WAVES)
+        def _():
+            start(z_copies(g + 3))
+            kv_start(g + 3)
+
+        @pl.when(g == 1)
+        def _():
+            ox_wait()
+            start(oz_copies())
+
         @pl.when(g + 2 < WAVES)
         def _():
-            start(z_copies(g + 2))
-            start(kv_copies(g + 2))
-            kv_own(g + 2).start()
-
-        @pl.when(g == 1)
-        def _():
-            start(zo_copies())
+            z_wait(g + 2)
+            start(x_copies(g + 2))
 
         @pl.when(g + 1 < WAVES)
         def _():
-            z_wait(g + 1)
-            start(x_copies(*wave(g + 1, x_s, x_r)))
-
-        @pl.when(g == 2)
-        def _():
-            zo_wait()
-            start(x_copies(*owave(xo_s, xo_r)))
-
-        x_wait(*wave(g, x_s, x_r))
-        start(xx_copies(*wave(g, xx_s, xx_r)))
+            x_wait(g + 1)
+            start(xx_copies(g + 1))
 
         @pl.when(g == 3)
         def _():
-            x_wait(*owave(xo_s, xo_r))
-            start(xx_copies(*owave(xxo_s, xxo_r)))
-
-        xx_wait(*wave(g, xx_s, xx_r))
+            oz_wait((2, 3))
+            start(ozz_copies())
+
+        xx_wait(g)
 
         for at in range(NX):
             heads = jnp.concatenate([w_buf[g, at, :, :, t].reshape(256, LANES) for t in range(3)], axis=1)
@@ -325,6 +343,17 @@
         fkv_copy(g).start()
         kv_wait(g)
 
+        @pl.when(g == WAVES - 1)
+        def _():
+            oz_wait((0, 1, 4, 5, 6, 7))
+            both_picks = jnp.concatenate([pick_a[...], pick_b[3]], axis=1)
+            for at in range(NX):
+                heads = [wo_buf[:, at, :, i].reshape(256, LANES) for i in range(WAVES)]
+                rest = [w_buf[i, at, :, :, 3].reshape(256, LANES) for i in range(WAVES)]
+                stack = jnp.concatenate([jnp.concatenate(heads, axis=1), jnp.concatenate(rest, axis=1)], axis=0)
+                wo_nat[core, at * 320 : (at + 1) * 320, :] = dot(both_picks, stack).astype(BF16)
+            won_copy().start()
+
         ho_out[g] = attend(g, 1)
         ho_copy(g).start()
         ho[core * WAVES + g] = attend(g, 0)
@@ -332,13 +361,6 @@
 
     lax.fori_loop(0, WAVES, step, 0)
 
-    xx_wait(*owave(xxo_s, xxo_r))
-    for at in range(NX):
-        for g in range(WAVES):
-            part = dot(pick_a[...], wo_buf[at, :, :, g].reshape(256, LANES))
-            part = part + dot(pick_b[3], w_buf[g, at, :, :, 3].reshape(256, LANES))
-            wo_nat[core, at * 320 : (at + 1) * 320, g * LANES : (g + 1) * LANES] = part.astype(BF16)
-    won_copy().start()
     for g in range(WAVES):
         ho_wait(g)
     there = wo_nat.at[1 - core]
@@ -347,15 +369,11 @@
     for i in range(2):
         att_ref[:, i * HALF : (i + 1) * HALF] = dot(lhs, wo_nat[i]).astype(BF16)
 
-    for copy in mom_copies() + y_copies() + zo_copies() + [nrm_copy(), won_copy()]:
+    for copy in mom_copies() + y_copies() + ox_copies() + oz_copies() + ozz_copies() + [nrm_copy(), won_copy()]:
         copy.wait_send()
-    for copy in x_copies(*owave(xo_s, xo_r)) + xx_copies(*owave(xxo_s, xxo_r)):
-        copy.wait_send()
 
     def drain(g, carry):
-        for copy in z_copies(g) + kv_copies(g) + [fkv_copy(g), ho_copy(g)]:
-            copy.wait_send()
-        for copy in x_copies(*wave(g, x_s, x_r)) + xx_copies(*wave(g, xx_s, xx_r)):
+        for copy in z_copies(g) + x_copies(g) + xx_copies(g) + kv_copies(g) + [fkv_copy(g), ho_copy(g)]:
             copy.wait_send()
         fkv_wait(g)
         fkv_own(g).wait()
@@ -381,7 +399,7 @@
         out_specs=(vmem, hbm, vmem, vmem),
         scratch_shapes=[
             pltpu.VMEM((WAVES, NX, NZ, NY, 4, 16, LANES), BF16),
-            pltpu.VMEM((NX, NZ, NY, WAVES, 16, LANES), BF16),
+            pltpu.VMEM((NZ, NX, NY, WAVES, 16, LANES), BF16),
             pltpu.VMEM((CH, 3 * LANES), BF16),
             pltpu.VMEM((2, CH, HALF), BF16),
             pltpu.VMEM((320, 256), BF16),
@@ -397,9 +415,8 @@
             dma((WAVES, z1)), dma((WAVES, z1)),
             dma((WAVES, 2)), dma((WAVES, 2)),
             dma((WAVES, 2)), dma((WAVES, 2)),
-            dma((z1,)), dma((z1,)),
-            dma((2,)), dma((2,)),
-            dma((2,)), dma((2,)),
+            dma((3,)), dma((3,)),
+            dma((8,)), dma((8,)),
             dma((WAVES, 3)), dma((WAVES, 3)), dma((WAVES,)),
             dma((3,)), dma((3,)),
             dma, dma,
@@ -413,7 +430,7 @@
         name="block",
     )(
         tokens.reshape(TOK, CH), stale_kv[0], stale_moments[0, 0],
-        norm_gain[None], norm_bias[None], w_query, w_key, w_value, w_out,
+        norm_gain, norm_bias, w_query, w_key, w_value, w_out,
     )
     return (
         attended.reshape(tokens.shape),

time: 126 us -> 90.1 us (0.72); the launches traced: 124 us -> 89.9 us
  Pallas kernels: 116 us -> 84.6 us
  local copies, waits for them, and re-layouts: 7.24 us -> 4.65 us
    pallas_call x1, Pallas kernels: 116 us -> 84.6 us  [shards(): pl.pallas_call(kernel, out_shape=(jax.ShapeDtypeStruct((TOK, CH), BF16),...]
    broadcast_in_dim x2 -> x0, local copies, waits for them, and re-layouts: 2.59 us -> none  [the longest x1 1.29 us: shards(): norm_gain[None]]
where the time goes in v2:
time: 90.1 us; the launch traced here: 89.9 us
  Pallas kernels  84.6 us (94%)
  local copies, waits for them, and re-layouts  4.65 us (5%)
    pallas_call x1, Pallas kernels, shards(): pl.pallas_call(kernel, out_shape=(jax.ShapeDtypeStruct((TOK, CH), BF16),...  84.6 us
    unnamed x10, local copies, waits for them, and re-layouts  4.65 us

profile of v2, /device:TPU:1, one launch (start us, length us, event | category | flops | bytes accessed | tf_op | source)
XLA Modules:
  0.0 89.9 jit_solution(16801617129896488731)
XLA Ops:
  0.6 84.6 %block.1 = (bf16[384,1280]{1,0:T(8,128)(2,1)}, bf16[2,384,1280]{2,1,0:T(8,128)(2,1)}, f32[1,32]{1,0:T(1,128)}, f32[1,32]{1,0:T(1,128)}) custom-call(bf16[384,1280]{1,0:T(8,128)(2,1)} %bitcast.9, bf16[2,384,1280]{2,1,0:T(8,128)(2,1)} %bitcast.7, f32[2,32]{1,0:T(2,128)} %bitcast.11, f32[1280]{0:T(1024)} %gain_ref.1, f32[1280]{0:T(1024)} %bias_ref.1, ...), custom_call_target="tpu_custom_call" | custom-call | tf_op jit(solution)/shard_map/block/pallas_call | solution.py:390
  85.3 0.0 copy-start
  85.3 2.4 %copy.17 = bf16[1,24,16,1280]{3,2,1,0:T(8,128)(2,1)} copy(bf16[1,24,16,1280]{3,2,1,0:T(8,128)(2,1)} %bitcast.10) | data formatting | bytes 1966080
  87.6 0.0 copy-done
  87.6 0.0 copy-start.2
  87.6 0.0 copy-start.1
  87.6 1.3 %copy.18 = bf16[1,2,384,1280]{3,2,1,0:T(8,128)(2,1)} copy(bf16[1,2,384,1280]{3,2,1,0:T(8,128)(2,1)S(1)} %bitcast.8) | data formatting | bytes 3932160
  88.9 0.0 copy-done.2
  88.9 0.5 copy.19
  89.4 0.0 copy-done.1
  89.4 0.5 copy.20
Async XLA Ops:
  85.3 2.4 %copy-start = (bf16[2,384,1280]{2,1,0:T(8,128)(2,1)S(1)}, bf16[2,384,1280]{2,1,0:T(8,128)(2,1)}, u32[]{:S(2)}) copy-start(bf16[2,384,1280]{2,1,0:T(8,128)(2,1)} %get-tuple-element.9) | copy-start | bytes 5898244
  87.6 1.3 %copy-start.2 = (f32[1,32]{1,0:T(1,128)S(1)}, f32[1,32]{1,0:T(1,128)}, u32[]{:S(2)}) copy-start(f32[1,32]{1,0:T(1,128)} %get-tuple-element.10) | copy-start | bytes 388
  87.6 1.8 %copy-start.1 = (f32[1,32]{1,0:T(1,128)S(1)}, f32[1,32]{1,0:T(1,128)}, u32[]{:S(2)}) copy-start(f32[1,32]{1,0:T(1,128)} %get-tuple-element.11) | copy-start | bytes 388

commit v3 on v2

--- a/solution.py
+++ b/solution.py
@@ -14,6 +14,8 @@
 HALF = 640
 LANES = 128
 WAVES = 5
+RING = 1
+DIRECT = WAVES - 1
 NX, NZ, NY = 4, 8, 2
 SHARD = 20
 GROUPS = 32
@@ -27,8 +29,8 @@
 def kernel(
     tok_ref, kv_ref, mom_ref, gain_ref, bias_ref, wq_ref, wk_ref, wv_ref, wo_ref,
     att_ref, fkv_ref, fs_ref, fq_ref,
-    w_buf, wo_buf, w_nat, wo_nat, pick_a, pick_b, tail, kvb, nrm, qb, ho, ho_out, moms,
-    y_s, y_r, z_s, z_r, x_s, x_r, xx_s, xx_r, ox_s, ox_r, oz_s, oz_r,
+    w_buf, b_buf, o_buf, w_nat, wo_nat, picks, part_pick, order, tail, kvb, nrm, qb, ho, ho_out, moms,
+    y_s, y_r, z_s, z_r, x_s, x_r, xx_s, xx_r, bx_s, bx_r, bz_s, bz_r, ox_s, ox_r, oz_s, oz_r,
     kv_s, kv_r, kv_l, mom_s, mom_r, nrm_s, nrm_r, fkv_s, fkv_r, fkv_l, ho_s, ho_r, won_s, won_r,
 ):
     row = lax.axis_index("rows")
@@ -43,7 +45,13 @@
     far = (row, (1 - yhi) * 2 + core)
     far_other = (row, (1 - yhi) * 2 + 1 - core)
     y_peer = (x * 16 + z * 2 + 1 - ylo, strip)
-    z_peers = [(x * 16 + ((z + d) % NZ) * 2 + ylo, strip) for d in range(1, NZ)]
+
+    def z_at(d):
+        return (z + NZ + d) % NZ
+
+    def z_peer(d):
+        return (x * 16 + z_at(d) * 2 + ylo, strip)
+
     xl = (x + NX - 1) % NX
     xr = (x + 1) % NX
     x_far = (x + 2) % NX
@@ -52,7 +60,7 @@
     x_across = (x_far * 16 + z * 2 + ylo, strip)
 
     barrier = pltpu.get_barrier_semaphore()
-    everyone = [sib, far, far_other, y_peer, x_left, x_right, x_across] + z_peers
+    everyone = [sib, far, far_other, y_peer, x_left, x_right, x_across] + [z_peer(d) for d in (1, -1, 2, -2)]
     for peer in everyone:
         pl.semaphore_signal(barrier, inc=1, device_id=peer, device_id_type=MESH)
 
@@ -66,79 +74,109 @@
         rows = ref[:, mine]
         for g in range(WAVES):
             piece = rows[:16, g * LANES : (g + 1) * LANES]
-            if t < 3:
-                w_buf[g, x, z, ylo, t] = piece
+            if t == 3:
+                o_buf[z, x, ylo, g] = piece
+            elif g == RING:
+                b_buf[z, x, ylo, t] = piece
             else:
-                wo_buf[z, x, ylo, g] = piece
+                w_buf[g - (g > RING), x, z, ylo, t] = piece
         tail[4 * t : 4 * t + 4, :] = rows.astype(F32)[16:SHARD, :]
     rest = tail[...].astype(BF16)
     for g in range(WAVES):
-        w_buf[g, x, z, ylo, 3] = rest[:, g * LANES : (g + 1) * LANES]
+        piece = rest[:, g * LANES : (g + 1) * LANES]
+        if g == RING:
+            b_buf[z, x, ylo, 3] = piece
+        else:
+            w_buf[g - (g > RING), x, z, ylo, 3] = piece
     moms[0] = jnp.zeros((8, LANES), F32)
     moms[0, 0:2, 0:GROUPS] = mom_ref[...]
 
     pl.semaphore_wait(barrier, len(everyone))
 
+    def y_refs(side):
+        return (
+            w_buf.at[0, x, z, side],
+            b_buf.at[z, x, side],
+            w_buf.at[pl.ds(1, DIRECT - 1), x, z, side],
+            o_buf.at[z, x, side],
+        )
+
     def y_copies():
-        here = w_buf.at[:, x, z, ylo]
-        ohere = wo_buf.at[z, x, ylo]
+        return [remote(ref, ref, y_s.at[i], y_r.at[i], y_peer) for i, ref in enumerate(y_refs(ylo))]
+
+    def y_wait(i):
+        there = y_refs(1 - ylo)[i]
+        remote(there, there, y_s.at[i], y_r.at[i], y_peer).wait_recv()
+
+    def z_copies(g):
+        here = w_buf.at[g, x, z]
         return [
-            remote(here, here, y_s.at[0], y_r.at[0], y_peer),
-            remote(ohere, ohere, y_s.at[1], y_r.at[1], y_peer),
+            remote(here, here, z_s.at[g, i], z_r.at[g, i], z_peer(d)) for i, d in enumerate((1, -1, 2, -2))
         ]
 
-    def y_wait():
-        there = w_buf.at[:, x, z, 1 - ylo]
-        othere = wo_buf.at[z, x, 1 - ylo]
-        remote(there, there, y_s.at[0], y_r.at[0], y_peer).wait_recv()
-        remote(othere, othere, y_s.at[1], y_r.at[1], y_peer).wait_recv()
-
-    def z_copies(g):
+    def zz_copies(g):
+        left, right = w_buf.at[g, x, z_at(-2)], w_buf.at[g, x, z_at(2)]
+        left_half, right_half = w_buf.at[g, x, z_at(-2), 0], w_buf.at[g, x, z_at(2), 1]
         return [
-            remote(w_buf.at[g, x, z], w_buf.at[g, x, z], z_s.at[g, d], z_r.at[g, d], z_peers[d])
-            for d in range(NZ - 1)
-        ]
-
-    def z_wait(g):
-        for d in range(NZ - 1):
-            there = w_buf.at[g, x, (z + NZ - 1 - d) % NZ]
-            remote(there, there, z_s.at[g, d], z_r.at[g, d], z_peers[d]).wait_recv()
-
-    def ox_copies():
-        here = wo_buf.at[z, x]
-        return [
-            remote(here, here, ox_s.at[i], ox_r.at[i], to) for i, to in enumerate((x_right, x_across, x_left))
-        ]
-
-    def ox_wait():
-        for i, at in enumerate((xl, x_far, xr)):
-            there = wo_buf.at[z, at]
-            remote(there, there, ox_s.at[i], ox_r.at[i], x_right).wait_recv()
-
-    def z_at(d):
-        return (z + NZ + d) % NZ
-
-    def z_peer(d):
-        return z_peers[(d - 1) % NZ]
-
-    def oz_copies():
-        here = wo_buf.at[z]
-        return [remote(here, here, oz_s.at[i], oz_r.at[i], z_peer(d)) for i, d in enumerate((1, -1, 2, -2))]
-
-    def ozz_copies():
-        left, right = wo_buf.at[z_at(-2)], wo_buf.at[z_at(2)]
-        left_half, right_half = wo_buf.at[z_at(-2), pl.ds(0, 2)], wo_buf.at[z_at(2), pl.ds(2, 2)]
-        return [
-            remote(ref, ref, oz_s.at[i + 4], oz_r.at[i + 4], z_peer(d))
+            remote(ref, ref, z_s.at[g, i + 4], z_r.at[g, i + 4], z_peer(d))
             for i, (ref, d) in enumerate(((left, 1), (right, -1), (left_half, 2), (right_half, -2)))
         ]
 
-    def oz_wait(which):
+    def z_wait(g, which):
         for i in which:
-            there = wo_buf.at[z_at((-1, 1, -2, 2, -3, 3, 4, 4)[i])]
-            if i >= 6:
-                there = wo_buf.at[z_at(4), pl.ds(2 * (i - 6), 2)]
-            remote(there, there, oz_s.at[i], oz_r.at[i], x_right).wait_recv()
+            there = w_buf.at[g, x, z_at((-1, 1, -2, 2, -3, 3)[i])] if i < 6 else w_buf.at[g, x, z_at(4), i - 6]
+            remote(there, there, z_s.at[g, i], z_r.at[g, i], x_right).wait_recv()
+
+    class Ring:
+        def __init__(self, buf, x_send, x_recv, send, recv):
+            self.buf, self.x_send, self.x_recv, self.send, self.recv = buf, x_send, x_recv, send, recv
+
+        def x_copies(self):
+            here = self.buf.at[z, x]
+            return [
+                remote(here, here, self.x_send.at[i], self.x_recv.at[i], to)
+                for i, to in enumerate((x_right, x_across, x_left))
+            ]
+
+        def x_wait(self):
+            for i, at in enumerate((xl, x_far, xr)):
+                there = self.buf.at[z, at]
+                remote(there, there, self.x_send.at[i], self.x_recv.at[i], x_right).wait_recv()
+
+        def refs(self, step):
+            if step < 3:
+                return self.buf.at[z_at(-1 - step)], self.buf.at[z_at(1 + step)]
+            return self.buf.at[z_at(4), pl.ds(0, 2)], self.buf.at[z_at(4), pl.ds(2, 2)]
+
+        def copies(self, step):
+            if step == 0:
+                refs = self.buf.at[z], self.buf.at[z]
+            elif step < 3:
+                refs = self.refs(step - 1)
+            else:
+                refs = self.buf.at[z_at(-3), pl.ds(0, 2)], self.buf.at[z_at(3), pl.ds(2, 2)]
+            return [
+                remote(ref, ref, self.send.at[2 * step + i], self.recv.at[2 * step + i], z_peer(d))
+                for i, (ref, d) in enumerate(zip(refs, (1, -1)))
+            ]
+
+        def wait(self, step):
+            for i, there in enumerate(self.refs(step)):
+                remote(there, there, self.send.at[2 * step + i], self.recv.at[2 * step + i], x_right).wait_recv()
+
+        def go(self, step):
+            if step == 0:
+                self.x_wait()
+            else:
+                self.wait(step - 1)
+            start(self.copies(step))
+
+        def drain(self):
+            for copy in self.x_copies() + [c for step in range(4) for c in self.copies(step)]:
+                copy.wait_send()
+
+    b_ring = Ring(b_buf, bx_s, bx_r, bz_s, bz_r)
+    o_ring = Ring(o_buf, ox_s, ox_r, oz_s, oz_r)
 
     def x_copies(g):
         here = w_buf.at[g, x]
@@ -223,6 +261,21 @@
     def kv_start(g):
         start(kv_copies(g))
         kv_own(g).start()
+
+    def za(g):
+        start(z_copies(g))
+
+    def zb(g):
+        z_wait(g, (2, 3))
+        start(zz_copies(g))
+
+    def xa(g):
+        z_wait(g, (0, 1, 4, 5, 6, 7))
+        start(x_copies(g))
+
+    def xb(g):
+        x_wait(g)
+        start(xx_copies(g))
 
     start(y_copies())
     start(mom_copies())
@@ -240,20 +293,26 @@
     fs_ref[...] = fresh[0:1, 0:GROUPS]
     fq_ref[...] = fresh[1:2, 0:GROUPS]
 
-    y_wait()
-    start(z_copies(0))
-    start(ox_copies())
+    y_wait(0)
+    za(0)
+    y_wait(1)
+    start(b_ring.x_copies())
     kv_start(1)
     kv_start(2)
-    start(z_copies(1))
-
-    k_at = lax.broadcasted_iota(jnp.int32, (320, 256), 0)
-    j_at = lax.broadcasted_iota(jnp.int32, (320, 256), 1)
-    base = (j_at >> 4) * SHARD
-    pick_a[...] = jnp.where(k_at == base + (j_at & 15), 1.0, 0.0).astype(BF16)
-    for t in range(4):
-        hit = (k_at == base + 16 + (j_at & 3)) & (((j_at >> 2) & 3) == t)
-        pick_b[t] = jnp.where(hit, 1.0, 0.0).astype(BF16)
+
+    k_at = lax.broadcasted_iota(jnp.int32, (HALF, HALF), 0)
+    j_at = lax.broadcasted_iota(jnp.int32, (HALF, HALF), 1)
+    first = (j_at >> 8) * 320 + ((j_at & 255) >> 4) * SHARD + (j_at & 15)
+    j_at = j_at - 512
+    last = (j_at >> 6) * 320 + ((j_at & 63) >> 2) * SHARD + 16 + (j_at & 3)
+    order[...] = jnp.where(k_at == jnp.where(j_at < 0, first, last), 1.0, 0.0).astype(BF16)
+    r_at = lax.broadcasted_iota(jnp.int32, (192, 256), 0)
+    j_at = lax.broadcasted_iota(jnp.int32, (192, 256), 1)
+    hit = j_at == ((r_at & 63) >> 2) * 16 + (r_at >> 6) * 4 + (r_at & 3)
+    part_pick[...] = jnp.where(hit, 1.0, 0.0).astype(BF16)
+
+    zb(0)
+    b_ring.go(0)
 
     for i in range(3):
         there = moms.at[i + 1]
@@ -268,16 +327,33 @@
     stats = jnp.where(inside, jnp.where(pick == 0, mean, jnp.where(pick == 1, rstd, 0.0)), 0.0)
     spread = dot(stats, member, dims=((1,), (1,)), precision=lax.Precision.HIGHEST)
     normed = (tok_ref[...].astype(F32) - spread[0:1, :]) * spread[1:2, :]
-    nrm[0:TOK, :] = (normed * gain_ref[...][None] + bias_ref[...][None]).astype(BF16)
+    normed = (normed * gain_ref[...][None] + bias_ref[...][None]).astype(BF16)
+    for i in range(2):
+        moved = dot(normed[:, i * HALF : (i + 1) * HALF], order[...]).astype(BF16)
+        nrm[0:TOK, i * 512 : (i + 1) * 512] = moved[:, :512]
+        nrm[0:TOK, 1024 + i * LANES : 1024 + (i + 1) * LANES] = moved[:, 512:]
     nrm_copy().start()
 
-    z_wait(0)
-    start(x_copies(0))
-    start(z_copies(2))
-    z_wait(1)
-    start(x_copies(1))
-    x_wait(0)
-    start(xx_copies(0))
+    xa(0)
+    y_wait(2)
+    y_wait(3)
+    za(1)
+    b_ring.go(1)
+    k_at = lax.broadcasted_iota(jnp.int32, (320, 256), 0)
+    j_at = lax.broadcasted_iota(jnp.int32, (320, 256), 1)
+    base = (j_at >> 4) * SHARD
+    picks[:, :256] = jnp.where(k_at == base + (j_at & 15), 1.0, 0.0).astype(BF16)
+    hit = (k_at == base + 16 + (j_at & 3)) & (((j_at >> 2) & 3) == 3)
+    picks[:, 256:] = jnp.where(hit, 1.0, 0.0).astype(BF16)
+    zb(1)
+    za(2)
+    b_ring.go(2)
+    xb(0)
+    xa(1)
+    zb(2)
+    b_ring.go(3)
+    za(3)
+    start(o_ring.x_copies())
     there = nrm.at[pl.ds(TOK, TOK)]
     remote(there, there, nrm_s, nrm_r, sib).wait_recv()
 
@@ -301,38 +377,47 @@
     def step(g, carry):
         @pl.when(g + 3 < WAVES)
         def _():
-            start(z_copies(g + 3))
             kv_start(g + 3)
 
-        @pl.when(g == 1)
-        def _():
-            ox_wait()
-            start(oz_copies())
-
-        @pl.when(g + 2 < WAVES)
-        def _():
-            z_wait(g + 2)
-            start(x_copies(g + 2))
-
-        @pl.when(g + 1 < WAVES)
-        def _():
-            x_wait(g + 1)
-            start(xx_copies(g + 1))
+        @pl.when(g == RING)
+        def _():
+            b_ring.wait(3)
+            o_ring.go(0)
+
+        @pl.when(g == 2)
+        def _():
+            xb(2)
+            xa(3)
+            o_ring.go(1)
 
         @pl.when(g == 3)
         def _():
-            oz_wait((2, 3))
-            start(ozz_copies())
-
-        xx_wait(g)
-
-        for at in range(NX):
-            heads = jnp.concatenate([w_buf[g, at, :, :, t].reshape(256, LANES) for t in range(3)], axis=1)
-            part = dot(pick_a[...], heads)
-            rest = w_buf[g, at, :, :, 3].reshape(256, LANES)
-            for t in range(3):
-                both = part[:, t * LANES : (t + 1) * LANES] + dot(pick_b[t], rest)
-                w_nat[at * 320 : (at + 1) * 320, t * LANES : (t + 1) * LANES] = both.astype(BF16)
+            o_ring.go(2)
+
+        at_wave = jnp.where(g > RING, g - 1, g)
+
+        @pl.when(g != RING)
+        def _():
+            xx_wait(at_wave)
+
+        def lay(tile):
+            for at in range(NX):
+                for t in range(3):
+                    w_nat[at * 256 : (at + 1) * 256, t * LANES : (t + 1) * LANES] = tile(at, t)
+                rows = dot(part_pick[...], tile(at, 3)).astype(BF16)
+                for t in range(3):
+                    w_nat[1024 + at * 64 : 1024 + (at + 1) * 64, t * LANES : (t + 1) * LANES] = rows[
+                        t * 64 : (t + 1) * 64
+                    ]
+
+        @pl.when(g != RING)
+        def _():
+            lay(lambda at, t: w_buf[at_wave, at, :, :, t].reshape(256, LANES))
+
+        @pl.when(g == RING)
+        def _():
+            lay(lambda at, t: b_buf[:, at, :, t].reshape(256, LANES))
+
         result = dot(nrm[...], w_nat[...])
         qb[...] = (result[:, :LANES] * 0.125).astype(BF16)
         for t in range(2):
@@ -345,17 +430,33 @@
 
         @pl.when(g == WAVES - 1)
         def _():
-            oz_wait((0, 1, 4, 5, 6, 7))
-            both_picks = jnp.concatenate([pick_a[...], pick_b[3]], axis=1)
+            o_ring.wait(3)
             for at in range(NX):
-                heads = [wo_buf[:, at, :, i].reshape(256, LANES) for i in range(WAVES)]
-                rest = [w_buf[i, at, :, :, 3].reshape(256, LANES) for i in range(WAVES)]
+                heads = [o_buf[:, at, :, i].reshape(256, LANES) for i in range(WAVES)]
+                rest = [
+                    b_buf[:, at, :, 3].reshape(256, LANES)
+                    if i == RING
+                    else w_buf[i - (i > RING), at, :, :, 3].reshape(256, LANES)
+                    for i in range(WAVES)
+                ]
                 stack = jnp.concatenate([jnp.concatenate(heads, axis=1), jnp.concatenate(rest, axis=1)], axis=0)
-                wo_nat[core, at * 320 : (at + 1) * 320, :] = dot(both_picks, stack).astype(BF16)
+                wo_nat[core, at * 320 : (at + 1) * 320, :] = dot(picks[...], stack).astype(BF16)
             won_copy().start()
 
         ho_out[g] = attend(g, 1)
         ho_copy(g).start()
+
+        @pl.when(g == 0)
+        def _():
+            xb(1)
+            zb(3)
+            xa(2)
+
+        @pl.when(g == 3)
+        def _():
+            xb(3)
+            o_ring.go(3)
+
         ho[core * WAVES + g] = attend(g, 0)
         return carry
 
@@ -369,11 +470,20 @@
     for i in range(2):
         att_ref[:, i * HALF : (i + 1) * HALF] = dot(lhs, wo_nat[i]).astype(BF16)
 
-    for copy in mom_copies() + y_copies() + ox_copies() + oz_copies() + ozz_copies() + [nrm_copy(), won_copy()]:
+    for copy in mom_copies() + y_copies() + [nrm_copy(), won_copy()]:
         copy.wait_send()
+    b_ring.drain()
+    o_ring.drain()
+
+    def drain_direct(g, carry):
+        for copy in z_copies(g) + zz_copies(g) + x_copies(g) + xx_copies(g):
+            copy.wait_send()
+        return carry
+
+    lax.fori_loop(0, DIRECT, drain_direct, 0)
 
     def drain(g, carry):
-        for copy in z_copies(g) + x_copies(g) + xx_copies(g) + kv_copies(g) + [fkv_copy(g), ho_copy(g)]:
+        for copy in kv_copies(g) + [fkv_copy(g), ho_copy(g)]:
             copy.wait_send()
         fkv_wait(g)
         fkv_own(g).wait()
@@ -386,7 +496,6 @@
     vmem = pl.BlockSpec(memory_space=pltpu.VMEM)
     hbm = pl.BlockSpec(memory_space=pl.ANY)
     dma = pltpu.SemaphoreType.DMA
-    z1 = NZ - 1
     attended, fresh_kv, sums, squares = pl.pallas_call(
         kernel,
         out_shape=(
@@ -398,12 +507,14 @@
         in_specs=[vmem, hbm] + [vmem] * 7,
         out_specs=(vmem, hbm, vmem, vmem),
         scratch_shapes=[
-            pltpu.VMEM((WAVES, NX, NZ, NY, 4, 16, LANES), BF16),
+            pltpu.VMEM((DIRECT, NX, NZ, NY, 4, 16, LANES), BF16),
+            pltpu.VMEM((NZ, NX, NY, 4, 16, LANES), BF16),
             pltpu.VMEM((NZ, NX, NY, WAVES, 16, LANES), BF16),
             pltpu.VMEM((CH, 3 * LANES), BF16),
             pltpu.VMEM((2, CH, HALF), BF16),
-            pltpu.VMEM((320, 256), BF16),
-            pltpu.VMEM((4, 320, 256), BF16),
+            pltpu.VMEM((320, 512), BF16),
+            pltpu.VMEM((192, 256), BF16),
+            pltpu.VMEM((HALF, HALF), BF16),
             pltpu.VMEM((16, HALF), F32),
             pltpu.VMEM((WAVES, 2, 6 * TOK, LANES), BF16),
             pltpu.VMEM((2 * TOK, CH), BF16),
@@ -411,10 +522,12 @@
             pltpu.VMEM((2 * WAVES, TOK, LANES), BF16),
             pltpu.VMEM((WAVES, TOK, LANES), BF16),
             pltpu.VMEM((4, 8, LANES), F32),
-            dma((2,)), dma((2,)),
-            dma((WAVES, z1)), dma((WAVES, z1)),
-            dma((WAVES, 2)), dma((WAVES, 2)),
-            dma((WAVES, 2)), dma((WAVES, 2)),
+            dma((4,)), dma((4,)),
+            dma((DIRECT, 8)), dma((DIRECT, 8)),
+            dma((DIRECT, 2)), dma((DIRECT, 2)),
+            dma((DIRECT, 2)), dma((DIRECT, 2)),
+            dma((3,)), dma((3,)),
+            dma((8,)), dma((8,)),
             dma((3,)), dma((3,)),
             dma((8,)), dma((8,)),
             dma((WAVES, 3)), dma((WAVES, 3)), dma((WAVES,)),

time: 90.1 us -> 82.1 us (0.911)
  Pallas kernels: 84.6 us -> 76.6 us
    pallas_call x1, Pallas kernels: 84.6 us -> 76.6 us  [shards(): pl.pallas_call(kernel, out_shape=(jax.ShapeDtypeStruct((TOK, CH), BF16),...]
where the time goes in v3:
time: 82.1 us; the launch traced here: 81.9 us
  Pallas kernels  76.6 us (93%)
  local copies, waits for them, and re-layouts  4.65 us (6%)
    pallas_call x1, Pallas kernels, shards(): pl.pallas_call(kernel, out_shape=(jax.ShapeDtypeStruct((TOK, CH), BF16),...  76.6 us
    unnamed x10, local copies, waits for them, and re-layouts  4.65 us

profile of v3, /device:TPU:1, one launch (start us, length us, event | category | flops | bytes accessed | tf_op | source)
XLA Modules:
  0.0 81.9 jit_solution(5325867177250049998)
XLA Ops:
  0.6 76.6 %block.1 = (bf16[384,1280]{1,0:T(8,128)(2,1)}, bf16[2,384,1280]{2,1,0:T(8,128)(2,1)}, f32[1,32]{1,0:T(1,128)}, f32[1,32]{1,0:T(1,128)}) custom-call(bf16[384,1280]{1,0:T(8,128)(2,1)} %bitcast.9, bf16[2,384,1280]{2,1,0:T(8,128)(2,1)} %bitcast.7, f32[2,32]{1,0:T(2,128)} %bitcast.11, f32[1280]{0:T(1024)} %gain_ref.1, f32[1280]{0:T(1024)} %bias_ref.1, ...), custom_call_target="tpu_custom_call" | custom-call | tf_op jit(solution)/shard_map/block/pallas_call | solution.py:499
  77.2 0.0 copy-start
  77.2 2.4 %copy.17 = bf16[1,24,16,1280]{3,2,1,0:T(8,128)(2,1)} copy(bf16[1,24,16,1280]{3,2,1,0:T(8,128)(2,1)} %bitcast.10) | data formatting | bytes 1966080
  79.6 0.0 copy-done
  79.6 0.0 copy-start.2
  79.6 0.0 copy-start.1
  79.6 1.3 %copy.18 = bf16[1,2,384,1280]{3,2,1,0:T(8,128)(2,1)} copy(bf16[1,2,384,1280]{3,2,1,0:T(8,128)(2,1)S(1)} %bitcast.8) | data formatting | bytes 3932160
  80.8 0.0 copy-done.2
  80.8 0.5 copy.19
  81.4 0.0 copy-done.1
  81.4 0.5 copy.20
Async XLA Ops:
  77.2 2.4 %copy-start = (bf16[2,384,1280]{2,1,0:T(8,128)(2,1)S(1)}, bf16[2,384,1280]{2,1,0:T(8,128)(2,1)}, u32[]{:S(2)}) copy-start(bf16[2,384,1280]{2,1,0:T(8,128)(2,1)} %get-tuple-element.9) | copy-start | bytes 5898244
  79.6 1.3 %copy-start.2 = (f32[1,32]{1,0:T(1,128)S(1)}, f32[1,32]{1,0:T(1,128)}, u32[]{:S(2)}) copy-start(f32[1,32]{1,0:T(1,128)} %get-tuple-element.10) | copy-start | bytes 388
  79.6 1.8 %copy-start.1 = (f32[1,32]{1,0:T(1,128)S(1)}, f32[1,32]{1,0:T(1,128)}, u32[]{:S(2)}) copy-start(f32[1,32]{1,0:T(1,128)} %get-tuple-element.11) | copy-start | bytes 388

commit v4 on v3

--- a/solution.py
+++ b/solution.py
@@ -499,13 +499,13 @@
     attended, fresh_kv, sums, squares = pl.pallas_call(
         kernel,
         out_shape=(
-            jax.ShapeDtypeStruct((TOK, CH), BF16),
-            jax.ShapeDtypeStruct((2, TOK, CH), BF16),
+            pltpu.VMEM((TOK, CH), BF16),
+            pltpu.VMEM((2, TOK, CH), BF16),
             jax.ShapeDtypeStruct((1, GROUPS), F32),
             jax.ShapeDtypeStruct((1, GROUPS), F32),
         ),
         in_specs=[vmem, hbm] + [vmem] * 7,
-        out_specs=(vmem, hbm, vmem, vmem),
+        out_specs=(vmem, vmem, vmem, vmem),
         scratch_shapes=[
             pltpu.VMEM((DIRECT, NX, NZ, NY, 4, 16, LANES), BF16),
             pltpu.VMEM((NZ, NX, NY, 4, 16, LANES), BF16),

time: 82.1 us -> 80.4 us (0.979)
  local copies, waits for them, and re-layouts: 4.65 us -> 3.25 us
    unnamed x10 -> x8, local copies, waits for them, and re-layouts: 4.65 us -> 3.25 us
where the time goes in v4:
time: 80.4 us; the launch traced here: 80 us
  Pallas kernels  76.1 us (95%)
  local copies, waits for them, and re-layouts  3.25 us (4%)
    pallas_call x1, Pallas kernels, shards(): pl.pallas_call(kernel, out_shape=(pltpu.VMEM((TOK, CH), BF16), pltpu.VMEM...  76.1 us
    unnamed x8, local copies, waits for them, and re-layouts  3.25 us

profile of v4, /device:TPU:1, one launch (start us, length us, event | category | flops | bytes accessed | tf_op | source)
XLA Modules:
  0.0 80.0 jit_solution(14675963966021491316)
XLA Ops:
  0.6 76.1 %block.1 = (bf16[384,1280]{1,0:T(8,128)(2,1)S(1)}, bf16[2,384,1280]{2,1,0:T(8,128)(2,1)S(1)}, f32[1,32]{1,0:T(1,128)}, f32[1,32]{1,0:T(1,128)}) custom-call(bf16[384,1280]{1,0:T(8,128)(2,1)} %bitcast.10, bf16[2,384,1280]{2,1,0:T(8,128)(2,1)} %bitcast.9, f32[2,32]{1,0:T(2,128)} %bitcast.11, f32[1280]{0:T(1024)} %gain_ref.1, f32[1280]{0:T(1024)} %bias_ref.1, ...), custom_call_target="tpu_custom_call" | custom-call | tf_op jit(solution)/shard_map/block/pallas_call | solution.py:499
  76.7 0.9 %copy.17 = bf16[1,24,16,1280]{3,2,1,0:T(8,128)(2,1)} copy(bf16[1,24,16,1280]{3,2,1,0:T(8,128)(2,1)S(1)} %bitcast.8) | data formatting | bytes 1966080
  77.7 0.0 copy-start.1
  77.7 0.0 copy-start
  77.7 1.3 %copy.18 = bf16[1,2,384,1280]{3,2,1,0:T(8,128)(2,1)} copy(bf16[1,2,384,1280]{3,2,1,0:T(8,128)(2,1)S(1)} %bitcast.7) | data formatting | bytes 3932160
  78.9 0.0 copy-done.1
  79.0 0.5 copy.19
  79.5 0.0 copy-done
  79.5 0.5 copy.20
Async XLA Ops:
  77.7 1.3 %copy-start.1 = (f32[1,32]{1,0:T(1,128)S(1)}, f32[1,32]{1,0:T(1,128)}, u32[]{:S(2)}) copy-start(f32[1,32]{1,0:T(1,128)} %get-tuple-element.10) | copy-start | bytes 388
  77.7 1.8 %copy-start = (f32[1,32]{1,0:T(1,128)S(1)}, f32[1,32]{1,0:T(1,128)}, u32[]{:S(2)}) copy-start(f32[1,32]{1,0:T(1,128)} %get-tuple-element.11) | copy-start | bytes 388
